TPU v7x, 512 devices: a whole 4x4x16 slice. The times are simulated.
512 devices in a mesh: snd: 32 (over y, x, core), rcv: 16 (over z).
Axes of the slice: x: 4, y: 4, z: 16, core: 2. Of those that a mesh axis runs over, the one named last changes fastest.
Arguments:
- nodes: bfloat16 [4096, 512], P(('snd', 'rcv')), may hold values from -6 to 6
- edges: bfloat16 [32, 16, 256, 512], P('snd', 'rcv'), may hold values from -6 to 6
- send_local: int32 [32, 16, 256], P('snd', 'rcv'), may hold values from 0 to 127
- recv_local: int32 [32, 16, 256], P('snd', 'rcv'), may hold values from 0 to 255
- edge_count: int32 [32, 16], P('snd', 'rcv'), may hold values from 32 to 256, as said below
- edge_w1: bfloat16 [1536, 512], replicated, may hold values from -0.15625 to 0.15625
- edge_w2: bfloat16 [512, 512], replicated, may hold values from -0.25 to 0.25
- node_w1: bfloat16 [1024, 512], replicated, may hold values from -0.1875 to 0.1875
- node_w2: bfloat16 [512, 512], replicated, may hold values from -0.25 to 0.25
- grad_nodes_out: bfloat16 [4096, 512], P(('snd', 'rcv')), may hold values from -6 to 6
- grad_edges_out: bfloat16 [32, 16, 256, 512], P('snd', 'rcv'), may hold values from -6 to 6
Outputs:
- grad_nodes: float32 [4096, 512], P(('snd', 'rcv'))
- grad_edges: float32 [32, 16, 256, 512], P('snd', 'rcv')
Inputs may be any that keep to these rules, and one draw needn't show every extreme that they name: Live edges of a tile fill its first edge_count slots; in every draw some tile has all 256 slots live.
All inputs are finite; a program needn't handle non-finite values.
Results may differ from a plain program's by a relative error of at most 0.019.
Values may be sent and summed in bfloat16 or wider, within the bound.
A program may use at most 64 MiB of HBM per device.

v0:
```python
import jax
import jax.numpy as jnp
from jax import lax
from jax.sharding import PartitionSpec as P


def swish_slope(pre_act):
    sigma = jax.nn.sigmoid(pre_act)
    return sigma * (1.0 + pre_act * (1.0 - sigma))


def layer_norm(values):
    center = values - jnp.mean(values, -1, keepdims=True)
    inv_scale = lax.rsqrt(jnp.mean(center * center, -1, keepdims=True) + 1e-05)
    return (center * inv_scale, inv_scale)


def norm_backward(upstream, normed, inv_scale):
    return inv_scale * (
        upstream
        - jnp.mean(upstream, -1, keepdims=True)
        - normed * jnp.mean(upstream * normed, -1, keepdims=True)
    )


def mlp_forward(inputs_cat, first_w, second_w):
    pre_act = jnp.dot(inputs_cat, first_w, preferred_element_type=jnp.float32)
    hidden = jax.nn.silu(pre_act).astype(jnp.bfloat16)
    output = jnp.dot(hidden, second_w, preferred_element_type=jnp.float32)
    normed, inv_scale = layer_norm(output)
    return (pre_act, normed, inv_scale)


def mlp_backward(upstream, pre_act, normed, inv_scale, first_w, second_w):
    grad_out = norm_backward(upstream, normed, inv_scale).astype(jnp.bfloat16)
    grad_hidden = jnp.dot(grad_out, second_w.T, preferred_element_type=jnp.float32)
    grad_pre = (grad_hidden * swish_slope(pre_act)).astype(jnp.bfloat16)
    return jnp.dot(grad_pre, first_w.T, preferred_element_type=jnp.float32)


def node_backward(node_feat, aggregate, upstream_bf, node_w1, node_w2):
    feat_width = node_feat.shape[1]
    inputs_cat = jnp.concatenate([node_feat, aggregate.astype(jnp.bfloat16)], 1)
    pre_act, normed, inv_scale = mlp_forward(inputs_cat, node_w1, node_w2)
    upstream = upstream_bf.astype(jnp.float32)
    grad_in = mlp_backward(upstream, pre_act, normed, inv_scale, node_w1, node_w2)
    return (upstream + grad_in[:, :feat_width], grad_in[:, feat_width:])


def select_cols(indices, offset, span_rows, dtype):
    columns = jnp.arange(span_rows, dtype=jnp.int32)[None, :]
    return (indices[:, None] - offset == columns).astype(dtype)


def fold_bf16(indices, shard_rows, offset):
    picker = select_cols(indices, offset, shard_rows.shape[0], jnp.bfloat16)
    return jnp.dot(picker, shard_rows, preferred_element_type=jnp.float32)


def scatter_term(indices, values, offset, span_rows):
    picker = select_cols(indices, offset, span_rows, jnp.float32)
    return jnp.dot(picker.T, values, precision=lax.Precision.HIGHEST)


def local(
    nodes,
    edges,
    send_local,
    recv_local,
    edge_count,
    edge_w1,
    edge_w2,
    node_w1,
    node_w2,
    grad_nodes_out,
    grad_edges_out,
):
    node_rows = nodes.shape[0]
    edge_slots = edges.shape[2]
    feat_width = edges.shape[3]
    edge_feat = edges[0, 0]
    send_idx = send_local[0, 0]
    recv_idx = recv_local[0, 0]
    live_mask = (jnp.arange(edge_slots, dtype=jnp.int32) < edge_count[0, 0]).astype(jnp.float32)[
        :, None
    ]
    sender_edge = fold_bf16(
        send_idx, lax.all_gather(nodes, "rcv", axis=0, tiled=True), jnp.int32(0)
    ).astype(jnp.bfloat16)
    group_nodes, group_upstream = (
        lax.all_gather(nodes, "snd", axis=0, tiled=True),
        lax.all_gather(grad_nodes_out, "snd", axis=0, tiled=True),
    )
    picker = select_cols(recv_idx, 0, group_nodes.shape[0], jnp.bfloat16)
    receiver_edge = jnp.dot(picker, group_nodes, preferred_element_type=jnp.float32).astype(
        jnp.bfloat16
    )
    inputs_cat = jnp.concatenate([edge_feat, sender_edge, receiver_edge], 1)
    pre_act, normed, inv_scale = mlp_forward(inputs_cat, edge_w1, edge_w2)
    picker_f32 = picker.astype(jnp.float32)
    partial_agg = jnp.dot(picker_f32.T, normed * live_mask, precision=lax.Precision.HIGHEST)
    aggregate = lax.psum(partial_agg.astype(jnp.bfloat16), "snd").astype(jnp.float32)
    direct_all, agg_grad_all = node_backward(
        group_nodes, aggregate, group_upstream, node_w1, node_w2
    )
    direct = lax.dynamic_slice_in_dim(direct_all, lax.axis_index("snd") * node_rows, node_rows, 0)
    agg_grad_edge = jnp.dot(picker_f32, agg_grad_all, precision=lax.Precision.HIGHEST)
    cotangent = grad_edges_out[0, 0].astype(jnp.float32)
    upstream = (cotangent + agg_grad_edge) * live_mask
    grad_in = mlp_backward(upstream, pre_act, normed, inv_scale, edge_w1, edge_w2)
    edge_grad = live_mask * cotangent + grad_in[:, :feat_width]
    send_part = grad_in[:, feat_width : 2 * feat_width]
    recv_part = grad_in[:, 2 * feat_width :]
    send_own = lax.psum_scatter(
        scatter_term(send_idx, send_part, jnp.int32(0), node_rows * lax.axis_size("rcv")).astype(
            jnp.bfloat16
        ),
        "rcv",
        scatter_dimension=0,
        tiled=True,
    ).astype(jnp.float32)
    recv_own = lax.psum_scatter(
        scatter_term(recv_idx, recv_part, jnp.int32(0), node_rows * lax.axis_size("snd")).astype(
            jnp.bfloat16
        ),
        "snd",
        scatter_dimension=0,
        tiled=True,
    ).astype(jnp.float32)
    return (direct + send_own + recv_own, edge_grad[None, None])


def solution(mesh):
    in_specs = (
        P(("snd", "rcv"), None),
        P("snd", "rcv", None, None),
        P("snd", "rcv", None),
        P("snd", "rcv", None),
        P("snd", "rcv"),
        P(),
        P(),
        P(),
        P(),
        P(("snd", "rcv"), None),
        P("snd", "rcv", None, None),
    )
    out_specs = (P(("snd", "rcv"), None), P("snd", "rcv", None, None))
    return jax.shard_map(local, mesh=mesh, in_specs=in_specs, out_specs=out_specs, check_vma=False)
```

profile of v0, /device:TPU:1, one launch (start us, length us, event | category | flops | bytes accessed | tf_op | source)
XLA Modules:
  0.0 393.2 jit_solution(5266284681063897507)
XLA Ops:
  7.2 30.2 %all_gather.11 = bf16[128,512]{1,0:T(8,128)(2,1)S(1)} all-gather(bf16[8,512]{1,0:T(8,128)(2,1)} %param.11), channel_id=1, replica_groups=mesh['snd'=32,'rcv'=16] {'rcv'}, dimensions={0}, use_global_device_ids=true | all-gather | bytes 139264 | tf_op jit(solution)/shard_map/all_gather | solution.py:88
  37.4 32.6 %all_gather.10 = bf16[256,512]{1,0:T(8,128)(2,1)S(1)} all-gather(bf16[8,512]{1,0:T(8,128)(2,1)} %param.11), channel_id=1, replica_groups=mesh['snd'=32,'rcv'=16] {'snd'}, dimensions={0}, use_global_device_ids=true | all-gather | bytes 270336 | tf_op jit(solution)/shard_map/all_gather | solution.py:91
  70.8 0.9 convolution_convert_fusion.3
  71.7 1.0 convolution_convert_fusion.2
  72.7 1.6 fusion.5
  74.3 0.4 fusion.69
  74.7 0.2 multiply_reduce_fusion.3
  74.9 0.1 copy-done.7
  75.1 1.3 convolution_convert_fusion.1
  76.5 24.1 %all_gather.9 = bf16[256,512]{1,0:T(8,128)(2,1)S(1)} all-gather(bf16[8,512]{1,0:T(8,128)(2,1)S(1)} %copy-done.3), channel_id=1, replica_groups=mesh['snd'=32,'rcv'=16] {'snd'}, dimensions={0}, use_global_device_ids=true | all-gather | bytes 270336 | tf_op jit(solution)/shard_map/all_gather | solution.py:92
  100.6 101.5 %all-reduce.2.cloned.1.call-done = bf16[256,512]{1,0:T(8,128)(2,1)} async-done(((bf16[256,512]{1,0:T(8,128)(2,1)}), bf16[256,512]{1,0:T(8,128)(2,1)}) %all-reduce.2.cloned.1.call-update) | async-done | bytes 262160 | tf_op jit(solution)/shard_map/psum | solution.py:102
  202.1 1.7 fusion.16
  203.9 1.6 fusion.70
  205.6 0.2 multiply_reduce_fusion.2
  205.8 0.2 convert_reduce_fusion
  206.1 3.4 fusion.4
  209.4 1.7 fusion.68
  211.1 3.3 fusion.3
  214.5 2.1 convolution_convert_fusion.4
  216.6 2.3 convolution_convert_fusion
  219.0 2.0 fusion.12
  221.0 52.8 %reduce-scatter.3.cloned.1.call-done = bf16[8,512]{1,0:T(8,128)(2,1)} async-done(((bf16[128,512]{1,0:T(8,128)(2,1)}), bf16[8,512]{1,0:T(8,128)(2,1)}) %reduce-scatter.3.cloned.1.call-update) | async-done | bytes 8208 | tf_op jit(solution)/shard_map/reduce_scatter | solution.py:114
  273.7 111.6 %reduce-scatter.5.cloned.1.call-done = bf16[8,512]{1,0:T(8,128)(2,1)} async-done(((bf16[256,512]{1,0:T(8,128)(2,1)}), bf16[8,512]{1,0:T(8,128)(2,1)}) %reduce-scatter.5.cloned.1.call-update) | async-done | bytes 8208 | tf_op jit(solution)/shard_map/reduce_scatter | solution.py:122
  385.3 1.3 fusion.61
  (32 shorter events, 0.3 us)
Async XLA Ops:
  7.2 65.5 %copy-start = (bf16[1536,512]{1,0:T(8,128)(2,1)S(1)}, bf16[1536,512]{1,0:T(8,128)(2,1)}, u32[]{:S(2)}) copy-start(bf16[1536,512]{1,0:T(8,128)(2,1)} %param.16) | copy-start | bytes 4718596
  7.2 195.0 %all-reduce.2.cloned.1.call-start = ((), (), s32[]{:S(2)}) async-start(), calls=%async_computation.2 | async-start | bytes 524288 | tf_op jit(solution)/shard_map/psum | solution.py:102
  72.7 1.6 copy-start.5
  74.3 0.8 copy-start.7
  74.3 0.8 copy-start.2
  74.3 2.2 copy-start.3
  76.4 197.3 %reduce-scatter.3.cloned.1.call-start = ((), (), s32[]{:S(2)}) async-start(), calls=%async_computation.3 | async-start | bytes 139264 | tf_op jit(solution)/shard_map/reduce_scatter | solution.py:114
  203.9 1.9 copy-start.6
  206.0 3.4 copy-start.1
  211.1 3.3 copy-start.4
  216.5 168.8 %reduce-scatter.5.cloned.1.call-start = ((), (), s32[]{:S(2)}) async-start(), calls=%async_computation.4 | async-start | bytes 270336 | tf_op jit(solution)/shard_map/reduce_scatter | solution.py:122
  218.9 166.4 %slice-start = ((f32[256,1024]{1,0:T(8,128)}), f32[256,512]{1,0:T(8,128)S(1)}, s32[]{:S(2)}) async-start(f32[256,1024]{1,0:T(8,128)} %fusion.4), calls=%async_computation.5 | async-start | bytes 1048576 | tf_op jit(solution)/shard_map/slice | solution.py:47
Sparse Core Ops, SparseCore 0:
  76.5 125.5 all-reduce.1
  216.7 57.0 reduce-scatter.2
  278.1 107.2 reduce-scatter.4
where the time goes:
time: 395 us; the launch traced here: 393 us
  waiting for transfers between devices  266 us (67%)
  blocking collectives  87 us (22%)
  matrix products  21.2 us (5%)
  between operations  14.6 us (4%)
  other arithmetic  4.08 us (1%)
    reduce_scatter x1, waiting for transfers between devices, local(): lax.psum_scatter(scatter_term(recv_idx, recv_part, jnp.int32(0), node_row...  112 us
    psum x1, waiting for transfers between devices, local(): lax.psum(partial_agg.astype(jnp.bfloat16), 'snd').astype(jnp.float32)  102 us
    reduce_scatter x1, waiting for transfers between devices, local(): lax.psum_scatter(scatter_term(send_idx, send_part, jnp.int32(0), node_row...  52.8 us
    all_gather x1, blocking collectives, local(): lax.all_gather(nodes, 'snd', axis=0, tiled=True)  32.6 us
    all_gather x1, blocking collectives, local(): lax.all_gather(nodes, 'rcv', axis=0, tiled=True)  30.2 us
    all_gather x1, blocking collectives, local(): lax.all_gather(grad_nodes_out, 'snd', axis=0, tiled=True)  24.1 us
  transfers between devices with their start and end apart: 3, of which 3 were waited for; matrix products, arithmetic and copies ran while one was open for 1% of the time, Pallas kernels for 0%

commit v1 on v0

v1 whole, which is shorter than its diff:
```python
import jax
import jax.numpy as jnp
from jax import lax
from jax.experimental import pallas as pl
from jax.experimental.pallas import tpu as pltpu
from jax.sharding import PartitionSpec as P

MESH = pl.DeviceIdType.MESH
F32 = jnp.float32
BF16 = jnp.bfloat16
CHUNK = 64


def dot(a, b):
    return jnp.dot(a, b, preferred_element_type=F32)


def dot_t(a, b):
    return lax.dot_general(a, b, (((1,), (1,)), ((), ())), preferred_element_type=F32)


def pack_blocks(rows):
    count, width = rows.shape[0] // 8, rows.shape[1]
    blocks = rows.reshape(count, 8, width)
    return jnp.concatenate(
        [blocks[:, :, : width // 2], blocks[:, :, width // 2 :]], axis=1
    ).astype(BF16)


def unpack_blocks(blocks):
    blocks = blocks.astype(F32)
    count, _, half = blocks.shape
    return jnp.concatenate(
        [blocks[:, :8, :].reshape(count * 8, half), blocks[:, 8:, :].reshape(count * 8, half)],
        axis=1,
    )


def unpack_sum(blocks):
    total = jnp.sum(blocks.astype(F32), axis=0)
    return jnp.concatenate([total[:8], total[8:]], axis=1)


def layer_norm(values):
    center = values - jnp.mean(values, -1, keepdims=True)
    inv_scale = lax.rsqrt(jnp.mean(center * center, -1, keepdims=True) + 1e-05)
    return center * inv_scale, inv_scale


def norm_backward(upstream, normed, inv_scale):
    return inv_scale * (
        upstream
        - jnp.mean(upstream, -1, keepdims=True)
        - normed * jnp.mean(upstream * normed, -1, keepdims=True)
    )


def make_kernel(n_snd, n_rcv):
    def kernel(
        count_ref,
        send_ref,
        recv_ref,
        nodes_ref,
        gno_ref,
        edges_hbm,
        geo_hbm,
        w1_hbm,
        w2_hbm,
        nw1_hbm,
        nw2_hbm,
        gnodes_ref,
        gedges_ref,
        edges,
        geo,
        w1,
        w2,
        nw1,
        nw2,
        node_blk,
        nodes_r,
        nodes_s,
        agg_out,
        agg_in,
        gagg_blk,
        gagg_in,
        rs_out,
        rs_in,
        rr_out,
        rr_in,
        pre,
        normed,
        inv,
        work,
        hid,
        slope,
        load_sem,
        send_sem,
        recv_sem,
    ):
        me_s = lax.axis_index("snd")
        me_r = lax.axis_index("rcv")
        n_edges = edges.shape[0]
        d = edges.shape[1]

        loads = [
            pltpu.make_async_copy(src, dst, load_sem.at[k])
            for k, (src, dst) in enumerate(
                [
                    (edges_hbm, edges),
                    (w1_hbm, w1),
                    (w2_hbm, w2),
                    (nw1_hbm, nw1),
                    (nw2_hbm, nw2),
                    (geo_hbm, geo),
                ]
            )
        ]
        for load in loads:
            load.start()

        barrier = pltpu.get_barrier_semaphore()

        def greet(axis, me, n):
            def body(step, carry):
                pl.semaphore_signal(
                    barrier,
                    inc=1,
                    device_id={axis: lax.rem(me + step, n)},
                    device_id_type=MESH,
                )
                return carry

            lax.fori_loop(1, n, body, 0)

        greet("rcv", me_r, n_rcv)
        greet("snd", me_s, n_snd)

        def send_all(axis, me, n, src_of, dst, k):
            def body(step, carry):
                other = lax.rem(me + step, n)
                pltpu.make_async_remote_copy(
                    src_ref=src_of(other),
                    dst_ref=dst.at[me],
                    send_sem=send_sem.at[k],
                    recv_sem=recv_sem.at[k],
                    device_id={axis: other},
                    device_id_type=MESH,
                ).start()
                return carry

            lax.fori_loop(1, n, body, 0)

        def wait_for(sem, buf, n, k):
            part = buf.at[pl.ds(0, n - 1)]
            pltpu.make_async_copy(part, part, sem.at[k]).wait()

        own = pack_blocks(nodes_ref[...].astype(F32))
        node_blk[...] = own[0]
        nodes_r[me_r] = own[0]
        nodes_s[me_s] = own[0]

        pl.semaphore_wait(barrier, n_snd + n_rcv - 2)
        send_all("rcv", me_r, n_rcv, lambda o: node_blk, nodes_r, 0)
        send_all("snd", me_s, n_snd, lambda o: node_blk, nodes_s, 1)

        live_row = lax.broadcasted_iota(jnp.int32, (1, n_edges), 1) < count_ref[0, 0]
        live_col = lax.broadcasted_iota(jnp.int32, (n_edges, 1), 0) < count_ref[0, 0]
        send_idx = jnp.where(live_row, send_ref[...], -1)
        recv_idx = jnp.where(live_row, recv_ref[...], -1)

        def picker(idx, rows):
            rows_iota = lax.broadcasted_iota(jnp.int32, (rows, n_edges), 0)
            return jnp.where(rows_iota == idx, 1.0, 0.0).astype(F32)

        put_s = picker(send_idx, n_rcv * 8)
        put_r = picker(recv_idx, n_snd * 8)
        take_s = put_s.T.astype(BF16)
        take_r = put_r.T.astype(BF16)
        put_s = put_s.astype(BF16)
        put_r = put_r.astype(BF16)

        loads[0].wait()
        loads[1].wait()
        pre[...] = dot(edges[...], w1[:d])

        wait_for(recv_sem, nodes_r, n_rcv, 0)
        sender = dot(take_s, unpack_blocks(nodes_r[...]).astype(BF16)).astype(BF16)
        pre[...] += dot(sender, w1[d : 2 * d])
        wait_for(recv_sem, nodes_s, n_snd, 1)
        receiver = dot(take_r, unpack_blocks(nodes_s[...]).astype(BF16)).astype(BF16)
        work[...] = dot(receiver, w1[2 * d :])
        for start in range(0, n_edges, CHUNK):
            rows = pl.ds(start, CHUNK)
            act = pre[rows] + work[rows]
            pre[rows] = act
            hid[rows] = (act * jax.nn.sigmoid(act)).astype(BF16)
        loads[2].wait()
        work[...] = dot(hid[...], w2[...])
        for start in range(0, n_edges, CHUNK):
            rows = pl.ds(start, CHUNK)
            out, scale = layer_norm(work[rows])
            normed[rows] = out
            inv[rows] = scale
            hid[rows] = out.astype(BF16)
        agg_out[...] = pack_blocks(dot(put_r, hid[...]))
        send_all("snd", me_s, n_snd, lambda o: agg_out.at[o], agg_in, 2)
        agg_in[me_s] = agg_out[me_s]

        loads[3].wait()
        loads[4].wait()
        loads[5].wait()
        node_pre = dot(nodes_ref[...], nw1[:d])
        for start in range(0, n_edges, CHUNK):
            rows = pl.ds(start, CHUNK)
            act = pre[rows]
            sigma = jax.nn.sigmoid(act)
            slope[rows] = sigma * (1.0 + act * (1.0 - sigma))

        wait_for(recv_sem, agg_in, n_snd, 2)
        aggregate = unpack_sum(agg_in[...]).astype(BF16)
        node_pre = node_pre + dot(aggregate, nw1[d:])
        sigma = jax.nn.sigmoid(node_pre)
        node_out = dot((node_pre * sigma).astype(BF16), nw2[...])
        node_normed, node_inv = layer_norm(node_out)
        gno = gno_ref[...].astype(F32)
        node_gout = norm_backward(gno, node_normed, node_inv).astype(BF16)
        node_gpre = (
            dot_t(node_gout, nw2[...]) * (sigma * (1.0 + node_pre * (1.0 - sigma)))
        ).astype(BF16)
        gagg = pack_blocks(dot_t(node_gpre, nw1[d:]))
        gagg_blk[...] = gagg[0]
        gagg_in[me_s] = gagg[0]
        send_all("snd", me_s, n_snd, lambda o: gagg_blk, gagg_in, 3)
        direct = gno + dot_t(node_gpre, nw1[:d])

        wait_for(recv_sem, gagg_in, n_snd, 3)
        work[...] = dot(take_r, unpack_blocks(gagg_in[...]).astype(BF16))
        for start in range(0, n_edges, CHUNK):
            rows = pl.ds(start, CHUNK)
            live = (
                lax.broadcasted_iota(jnp.int32, (CHUNK, 1), 0) + start < count_ref[0, 0]
            )
            up = work[rows] + jnp.where(live, geo[rows].astype(F32), 0.0)
            hid[rows] = norm_backward(up, normed[rows], inv[rows]).astype(BF16)
        work[...] = dot_t(hid[...], w2[...])
        for start in range(0, n_edges, CHUNK):
            rows = pl.ds(start, CHUNK)
            hid[rows] = (work[rows] * slope[rows]).astype(BF16)
        send_part = dot_t(hid[...], w1[d : 2 * d]).astype(BF16)
        rs_out[...] = pack_blocks(dot(put_s, send_part))
        send_all("rcv", me_r, n_rcv, lambda o: rs_out.at[o], rs_in, 4)
        rs_in[me_r] = rs_out[me_r]
        recv_part = dot_t(hid[...], w1[2 * d :]).astype(BF16)
        rr_out[...] = pack_blocks(dot(put_r, recv_part))
        send_all("snd", me_s, n_snd, lambda o: rr_out.at[o], rr_in, 5)
        rr_in[me_s] = rr_out[me_s]
        gedges_ref[...] = jnp.where(live_col, geo[...].astype(F32), 0.0) + dot_t(
            hid[...], w1[:d]
        )

        wait_for(recv_sem, rr_in, n_snd, 5)
        direct = direct + unpack_sum(rr_in[...])
        wait_for(recv_sem, rs_in, n_rcv, 4)
        gnodes_ref[...] = direct + unpack_sum(rs_in[...])

        wait_for(send_sem, nodes_r, n_rcv, 0)
        wait_for(send_sem, nodes_s, n_snd, 1)
        wait_for(send_sem, agg_in, n_snd, 2)
        wait_for(send_sem, gagg_in, n_snd, 3)
        wait_for(send_sem, rs_in, n_rcv, 4)
        wait_for(send_sem, rr_in, n_snd, 5)

    return kernel


def solution(mesh):
    n_snd, n_rcv = mesh.shape["snd"], mesh.shape["rcv"]

    def local(
        nodes,
        edges,
        send_local,
        recv_local,
        edge_count,
        edge_w1,
        edge_w2,
        node_w1,
        node_w2,
        grad_nodes_out,
        grad_edges_out,
    ):
        n_edges, d = edges.shape[2:]
        vmem = pl.BlockSpec(memory_space=pltpu.VMEM)
        hbm = pl.BlockSpec(memory_space=pltpu.HBM)
        smem = pl.BlockSpec(memory_space=pltpu.SMEM)
        half = d // 2
        grad_nodes, grad_edges = pl.pallas_call(
            make_kernel(n_snd, n_rcv),
            out_shape=(
                jax.ShapeDtypeStruct(nodes.shape, F32),
                jax.ShapeDtypeStruct((n_edges, d), F32),
            ),
            in_specs=[smem, vmem, vmem, vmem, vmem] + [hbm] * 6,
            out_specs=(vmem, vmem),
            scratch_shapes=[
                pltpu.VMEM((n_edges, d), BF16),
                pltpu.VMEM((n_edges, d), BF16),
                pltpu.VMEM(edge_w1.shape, BF16),
                pltpu.VMEM(edge_w2.shape, BF16),
                pltpu.VMEM(node_w1.shape, BF16),
                pltpu.VMEM(node_w2.shape, BF16),
                pltpu.VMEM((16, half), BF16),
                pltpu.VMEM((n_rcv, 16, half), BF16),
                pltpu.VMEM((n_snd, 16, half), BF16),
                pltpu.VMEM((n_snd, 16, half), BF16),
                pltpu.VMEM((n_snd, 16, half), BF16),
                pltpu.VMEM((16, half), BF16),
                pltpu.VMEM((n_snd, 16, half), BF16),
                pltpu.VMEM((n_rcv, 16, half), BF16),
                pltpu.VMEM((n_rcv, 16, half), BF16),
                pltpu.VMEM((n_snd, 16, half), BF16),
                pltpu.VMEM((n_snd, 16, half), BF16),
                pltpu.VMEM((n_edges, d), F32),
                pltpu.VMEM((n_edges, d), F32),
                pltpu.VMEM((n_edges, 1), F32),
                pltpu.VMEM((n_edges, d), F32),
                pltpu.VMEM((n_edges, d), BF16),
                pltpu.VMEM((n_edges, d), F32),
                pltpu.SemaphoreType.DMA((6,)),
                pltpu.SemaphoreType.DMA((6,)),
                pltpu.SemaphoreType.DMA((6,)),
            ],
            compiler_params=pltpu.CompilerParams(
                collective_id=0, has_side_effects=True, vmem_limit_bytes=48 * 1024 * 1024
            ),
        )(
            edge_count,
            send_local.reshape(1, n_edges),
            recv_local.reshape(1, n_edges),
            nodes,
            grad_nodes_out,
            edges.reshape(n_edges, d),
            grad_edges_out.reshape(n_edges, d),
            edge_w1,
            edge_w2,
            node_w1,
            node_w2,
        )
        return grad_nodes, grad_edges.reshape(1, 1, n_edges, d)

    in_specs = (
        P(("snd", "rcv"), None),
        P("snd", "rcv", None, None),
        P("snd", "rcv", None),
        P("snd", "rcv", None),
        P("snd", "rcv"),
        P(),
        P(),
        P(),
        P(),
        P(("snd", "rcv"), None),
        P("snd", "rcv", None, None),
    )
    out_specs = (P(("snd", "rcv"), None), P("snd", "rcv", None, None))
    return jax.shard_map(local, mesh=mesh, in_specs=in_specs, out_specs=out_specs, check_vma=False)
```

time: 395 us -> 66.3 us (0.17)
  waiting for transfers between devices: 266 us -> 0 us
  blocking collectives: 87 us -> 0 us
  Pallas kernels: 0 us -> 53.6 us
  matrix products: 21.2 us -> 0 us
  between operations: 14.6 us -> 1.31 us
  local copies, waits for them, and re-layouts: 0.2 us -> 10.8 us
  other arithmetic: 4.08 us -> 0 us
    reduce_scatter x2 -> x0, waiting for transfers between devices: 164 us -> none  [the longest x1 112 us: local(): lax.psum_scatter(scatter_term(recv_idx, recv_part, jnp.int32(0), node_row...]
    psum x1 -> x0, waiting for transfers between devices: 102 us -> none  [local(): lax.psum(partial_agg.astype(jnp.bfloat16), 'snd').astype(jnp.float32)]
    all_gather x3 -> x0, blocking collectives: 87 us -> none  [the longest x1 32.6 us: local(): lax.all_gather(nodes, 'snd', axis=0, tiled=True)]
    pallas_call x0 -> x1, Pallas kernels: none -> 53.6 us  [local(): pl.pallas_call(make_kernel(n_snd, n_rcv), out_shape=(jax.ShapeDtypeStruct...]
    dot_general x12 -> x0, matrix products: 21.2 us -> none  [the longest x2 6.67 us: mlp_backward(): return jnp.dot(grad_pre, first_w.T, preferred_element_type=jnp.float32)]
    unnamed x16 -> x22, local copies, waits for them, and re-layouts: 0.2 us -> 10.8 us
  transfers between devices with their start and end apart: 3 -> 0, of which waited for: 3 -> 0; matrix products, arithmetic and copies ran while one was open for 1% -> 0% of each run, Pallas kernels for 0% -> 0%
where the time goes in v1:
time: 66.3 us; the launch traced here: 65.7 us
  Pallas kernels  53.6 us (81%)
  local copies, waits for them, and re-layouts  10.8 us (16%)
  between operations  1.31 us (2%)
    pallas_call x1, Pallas kernels, local(): pl.pallas_call(make_kernel(n_snd, n_rcv), out_shape=(jax.ShapeDtypeStruct...  53.6 us
    unnamed x22, local copies, waits for them, and re-layouts  10.8 us

profile of v1, /device:TPU:1, one launch (start us, length us, event | category | flops | bytes accessed | tf_op | source)
XLA Modules:
  0.0 65.7 jit_solution(10360264579839684862)
XLA Ops:
  1.3 0.0 copy-start
  1.3 1.4 %copy-done = bf16[1536,512]{1,0:T(8,128)(2,1)S(1)} copy-done((bf16[1536,512]{1,0:T(8,128)(2,1)S(1)}, bf16[1536,512]{1,0:T(8,128)(2,1)}, u32[]{:S(2)}) %copy-start) | copy-done | bytes 1572888
  2.7 0.0 copy-start.1
  2.7 1.2 %copy-done.1 = bf16[1024,512]{1,0:T(8,128)(2,1)S(1)} copy-done((bf16[1024,512]{1,0:T(8,128)(2,1)S(1)}, bf16[1024,512]{1,0:T(8,128)(2,1)}, u32[]{:S(2)}) %copy-start.1) | copy-done | bytes 1048600
  3.9 0.0 copy-start.2
  3.9 1.0 %copy-done.2 = bf16[512,512]{1,0:T(8,128)(2,1)S(1)} copy-done((bf16[512,512]{1,0:T(8,128)(2,1)S(1)}, bf16[512,512]{1,0:T(8,128)(2,1)}, u32[]{:S(2)}) %copy-start.2) | copy-done | bytes 524312
  5.0 0.0 copy-start.3
  5.0 1.0 %copy-done.3 = bf16[512,512]{1,0:T(8,128)(2,1)S(1)} copy-done((bf16[512,512]{1,0:T(8,128)(2,1)S(1)}, bf16[512,512]{1,0:T(8,128)(2,1)}, u32[]{:S(2)}) %copy-start.3) | copy-done | bytes 524312
  6.0 0.0 copy-start.4
  6.0 0.9 %copy-done.4 = bf16[1,1,256,512]{3,2,1,0:T(8,128)(2,1)S(1)} copy-done((bf16[1,1,256,512]{3,2,1,0:T(8,128)(2,1)S(1)}, bf16[1,1,256,512]{3,2,1,0:T(8,128)(2,1)}, u32[]{:S(2)}) %copy-start.4) | copy-done | bytes 262168
  6.9 0.0 copy-start.5
  7.0 0.9 %copy-done.5 = bf16[1,1,256,512]{3,2,1,0:T(8,128)(2,1)S(1)} copy-done((bf16[1,1,256,512]{3,2,1,0:T(8,128)(2,1)S(1)}, bf16[1,1,256,512]{3,2,1,0:T(8,128)(2,1)}, u32[]{:S(2)}) %copy-start.5) | copy-done | bytes 262168
  7.9 0.0 copy-start.6
  7.9 0.7 %copy-done.6 = bf16[8,512]{1,0:T(8,128)(2,1)S(1)} copy-done((bf16[8,512]{1,0:T(8,128)(2,1)S(1)}, bf16[8,512]{1,0:T(8,128)(2,1)}, u32[]{:S(2)}) %copy-start.6) | copy-done | bytes 8216
  8.6 0.0 copy-start.7
  8.6 0.7 %copy-done.7 = bf16[8,512]{1,0:T(8,128)(2,1)S(1)} copy-done((bf16[8,512]{1,0:T(8,128)(2,1)S(1)}, bf16[8,512]{1,0:T(8,128)(2,1)}, u32[]{:S(2)}) %copy-start.7) | copy-done | bytes 8216
  9.3 0.0 copy-start.8
  9.3 0.7 %copy-done.8 = s32[1,1,256]{2,1,0:T(1,128)S(1)} copy-done((s32[1,1,256]{2,1,0:T(1,128)S(1)}, s32[1,1,256]{2,1,0:T(1,128)}, u32[]{:S(2)}) %copy-start.8) | copy-done | bytes 1048
  10.0 0.0 copy-start.9
  10.0 0.7 %copy-done.9 = s32[1,1,256]{2,1,0:T(1,128)S(1)} copy-done((s32[1,1,256]{2,1,0:T(1,128)S(1)}, s32[1,1,256]{2,1,0:T(1,128)}, u32[]{:S(2)}) %copy-start.9) | copy-done | bytes 1048
  10.7 53.6 %shard_map.122 = (f32[8,512]{1,0:T(8,128)S(1)}, f32[256,512]{1,0:T(8,128)S(1)}) custom-call(s32[1,1]{1,0:T(1,128)S(6)} %copy.15.count_ref, s32[1,256]{1,0:T(1,128)S(1)} %bitcast.8, s32[1,256]{1,0:T(1,128)S(1)} %bitcast.9, bf16[8,512]{1,0:T(8,128)(2,1)S(1)} %copy-done.6, bf16[8,512]{1,0:T(8,128)(2,1)S(1)} %copy-done.7, bf16[256,512]{1,0:T(8,128)(2,1)S(1)} %bitcast.6, ...), custom_call_target="tpu_custom_call" | custom-call | tf_op jit(solution)/shard_map/pallas_call | solution.py:297
  64.3 0.6 copy.16
  64.9 0.8 %copy.17 = f32[1,1,256,512]{3,2,1,0:T(8,128)} copy(f32[1,1,256,512]{3,2,1,0:T(8,128)S(1)} %bitcast.5) | data formatting | bytes 1048576
Async XLA Ops:
  1.3 1.4 %copy-start = (bf16[1536,512]{1,0:T(8,128)(2,1)S(1)}, bf16[1536,512]{1,0:T(8,128)(2,1)}, u32[]{:S(2)}) copy-start(bf16[1536,512]{1,0:T(8,128)(2,1)} %w1_hbm.1) | copy-start | bytes 4718596
  2.7 1.2 %copy-start.1 = (bf16[1024,512]{1,0:T(8,128)(2,1)S(1)}, bf16[1024,512]{1,0:T(8,128)(2,1)}, u32[]{:S(2)}) copy-start(bf16[1024,512]{1,0:T(8,128)(2,1)} %nw1_hbm.1) | copy-start | bytes 3145732
  3.9 1.0 %copy-start.2 = (bf16[512,512]{1,0:T(8,128)(2,1)S(1)}, bf16[512,512]{1,0:T(8,128)(2,1)}, u32[]{:S(2)}) copy-start(bf16[512,512]{1,0:T(8,128)(2,1)} %w2_hbm.1) | copy-start | bytes 1572868
  5.0 1.0 %copy-start.3 = (bf16[512,512]{1,0:T(8,128)(2,1)S(1)}, bf16[512,512]{1,0:T(8,128)(2,1)}, u32[]{:S(2)}) copy-start(bf16[512,512]{1,0:T(8,128)(2,1)} %nw2_hbm.1) | copy-start | bytes 1572868
  6.0 0.9 %copy-start.4 = (bf16[1,1,256,512]{3,2,1,0:T(8,128)(2,1)S(1)}, bf16[1,1,256,512]{3,2,1,0:T(8,128)(2,1)}, u32[]{:S(2)}) copy-start(bf16[1,1,256,512]{3,2,1,0:T(8,128)(2,1)} %param.12) | copy-start | bytes 786436
  6.9 0.9 %copy-start.5 = (bf16[1,1,256,512]{3,2,1,0:T(8,128)(2,1)S(1)}, bf16[1,1,256,512]{3,2,1,0:T(8,128)(2,1)}, u32[]{:S(2)}) copy-start(bf16[1,1,256,512]{3,2,1,0:T(8,128)(2,1)} %param.21) | copy-start | bytes 786436
  7.9 0.7 %copy-start.6 = (bf16[8,512]{1,0:T(8,128)(2,1)S(1)}, bf16[8,512]{1,0:T(8,128)(2,1)}, u32[]{:S(2)}) copy-start(bf16[8,512]{1,0:T(8,128)(2,1)} %nodes_ref.1) | copy-start | bytes 24580
  8.6 0.7 %copy-start.7 = (bf16[8,512]{1,0:T(8,128)(2,1)S(1)}, bf16[8,512]{1,0:T(8,128)(2,1)}, u32[]{:S(2)}) copy-start(bf16[8,512]{1,0:T(8,128)(2,1)} %gno_ref.1) | copy-start | bytes 24580
  9.3 0.7 %copy-start.8 = (s32[1,1,256]{2,1,0:T(1,128)S(1)}, s32[1,1,256]{2,1,0:T(1,128)}, u32[]{:S(2)}) copy-start(s32[1,1,256]{2,1,0:T(1,128)} %param.13) | copy-start | bytes 3076
  10.0 0.7 %copy-start.9 = (s32[1,1,256]{2,1,0:T(1,128)S(1)}, s32[1,1,256]{2,1,0:T(1,128)}, u32[]{:S(2)}) copy-start(s32[1,1,256]{2,1,0:T(1,128)} %param.14) | copy-start | bytes 3076

commit v2 on v1

--- a/solution.py
+++ b/solution.py
@@ -1,3 +1,5 @@
+import itertools
+
 import jax
 import jax.numpy as jnp
 from jax import lax
@@ -56,12 +58,14 @@
 
 
 def make_kernel(n_snd, n_rcv):
+    far_first = sorted(range(1, n_rcv), key=lambda step: -min(step, n_rcv - step))
+
     def kernel(
-        count_ref,
-        send_ref,
-        recv_ref,
-        nodes_ref,
-        gno_ref,
+        count_hbm,
+        send_hbm,
+        recv_hbm,
+        nodes_hbm,
+        gno_hbm,
         edges_hbm,
         geo_hbm,
         w1_hbm,
@@ -70,6 +74,11 @@
         nw2_hbm,
         gnodes_ref,
         gedges_ref,
+        count_ref,
+        send_ref,
+        recv_ref,
+        nodes_ref,
+        gno_ref,
         edges,
         geo,
         w1,
@@ -93,9 +102,14 @@
         work,
         hid,
         slope,
+        put_s,
+        put_r,
+        take_s,
+        take_r,
         load_sem,
         send_sem,
         recv_sem,
+        plane_sem,
     ):
         me_s = lax.axis_index("snd")
         me_r = lax.axis_index("rcv")
@@ -106,12 +120,17 @@
             pltpu.make_async_copy(src, dst, load_sem.at[k])
             for k, (src, dst) in enumerate(
                 [
+                    (nodes_hbm, nodes_ref),
+                    (count_hbm, count_ref),
+                    (send_hbm, send_ref),
+                    (recv_hbm, recv_ref),
                     (edges_hbm, edges),
                     (w1_hbm, w1),
                     (w2_hbm, w2),
                     (nw1_hbm, nw1),
                     (nw2_hbm, nw2),
                     (geo_hbm, geo),
+                    (gno_hbm, gno_ref),
                 ]
             )
         ]
@@ -120,81 +139,128 @@
 
         barrier = pltpu.get_barrier_semaphore()
 
-        def greet(axis, me, n):
-            def body(step, carry):
-                pl.semaphore_signal(
-                    barrier,
-                    inc=1,
-                    device_id={axis: lax.rem(me + step, n)},
-                    device_id_type=MESH,
-                )
-                return carry
-
-            lax.fori_loop(1, n, body, 0)
-
-        greet("rcv", me_r, n_rcv)
-        greet("snd", me_s, n_snd)
-
-        def send_all(axis, me, n, src_of, dst, k):
-            def body(step, carry):
-                other = lax.rem(me + step, n)
+        def plane(step):
+            return (me_r + step + n_rcv) % n_rcv
+
+        cores = [me_s % 2, (me_s + 1) % 2]
+        columns = [(me_s // 2 + dx) % 4 * 2 for dx in range(4)]
+        lines = [(me_s // 8 + dy) % 4 * 8 for dy in range(4)]
+        snd_partners = [
+            lines[dy] + columns[dx] + cores[core]
+            for dy, dx, core in sorted(
+                itertools.product(range(4), range(4), range(2)),
+                key=lambda step: -min(step[0], 4 - step[0]) - min(step[1], 4 - step[1]) - step[2] / 2,
+            )[:-1]
+        ]
+
+        for other in snd_partners:
+            pl.semaphore_signal(barrier, inc=1, device_id={"snd": other}, device_id_type=MESH)
+
+        near = (4, -4, 3, -3, 2, -2, 1, -1)
+        for step in near:
+            pl.semaphore_signal(
+                barrier, inc=1, device_id={"rcv": plane(step)}, device_id_type=MESH
+            )
+
+        def copy_snd(other, src, dst, k):
+            return pltpu.make_async_remote_copy(
+                src_ref=src,
+                dst_ref=dst.at[me_s],
+                send_sem=send_sem.at[k],
+                recv_sem=recv_sem.at[k],
+                device_id={"snd": other},
+                device_id_type=MESH,
+            )
+
+        def send_snd(src_of, dst, k):
+            for other in snd_partners:
+                copy_snd(other, src_of(other), dst, k).start()
+
+        def send_rcv(src_of, dst, k):
+            for step in far_first:
+                other = (me_r + step) % n_rcv
                 pltpu.make_async_remote_copy(
                     src_ref=src_of(other),
-                    dst_ref=dst.at[me],
+                    dst_ref=dst.at[me_r],
                     send_sem=send_sem.at[k],
                     recv_sem=recv_sem.at[k],
-                    device_id={axis: other},
+                    device_id={"rcv": other},
                     device_id_type=MESH,
                 ).start()
-                return carry
-
-            lax.fori_loop(1, n, body, 0)
+
+        def copy_plane(src, block, other):
+            return pltpu.make_async_remote_copy(
+                src_ref=src,
+                dst_ref=nodes_r.at[block],
+                send_sem=send_sem.at[0],
+                recv_sem=plane_sem.at[block],
+                device_id={"rcv": other},
+                device_id_type=MESH,
+            )
+
+        def wait_plane(block):
+            pltpu.make_async_copy(node_blk, nodes_r.at[block], plane_sem.at[block]).wait()
 
         def wait_for(sem, buf, n, k):
             part = buf.at[pl.ds(0, n - 1)]
             pltpu.make_async_copy(part, part, sem.at[k]).wait()
 
+        loads[0].wait()
         own = pack_blocks(nodes_ref[...].astype(F32))
         node_blk[...] = own[0]
         nodes_r[me_r] = own[0]
         nodes_s[me_s] = own[0]
 
-        pl.semaphore_wait(barrier, n_snd + n_rcv - 2)
-        send_all("rcv", me_r, n_rcv, lambda o: node_blk, nodes_r, 0)
-        send_all("snd", me_s, n_snd, lambda o: node_blk, nodes_s, 1)
-
-        live_row = lax.broadcasted_iota(jnp.int32, (1, n_edges), 1) < count_ref[0, 0]
-        live_col = lax.broadcasted_iota(jnp.int32, (n_edges, 1), 0) < count_ref[0, 0]
-        send_idx = jnp.where(live_row, send_ref[...], -1)
-        recv_idx = jnp.where(live_row, recv_ref[...], -1)
-
-        def picker(idx, rows):
-            rows_iota = lax.broadcasted_iota(jnp.int32, (rows, n_edges), 0)
-            return jnp.where(rows_iota == idx, 1.0, 0.0).astype(F32)
-
-        put_s = picker(send_idx, n_rcv * 8)
-        put_r = picker(recv_idx, n_snd * 8)
-        take_s = put_s.T.astype(BF16)
-        take_r = put_r.T.astype(BF16)
-        put_s = put_s.astype(BF16)
-        put_r = put_r.astype(BF16)
-
-        loads[0].wait()
-        loads[1].wait()
-        pre[...] = dot(edges[...], w1[:d])
-
-        wait_for(recv_sem, nodes_r, n_rcv, 0)
-        sender = dot(take_s, unpack_blocks(nodes_r[...]).astype(BF16)).astype(BF16)
-        pre[...] += dot(sender, w1[d : 2 * d])
+        def prepare():
+            loads[1].wait()
+            loads[2].wait()
+            loads[3].wait()
+            count = count_ref[...]
+            live_row = lax.broadcasted_iota(jnp.int32, (1, n_edges), 1) < count
+            send_idx = jnp.where(live_row, send_ref[...], -1)
+            recv_idx = jnp.where(live_row, recv_ref[...], -1)
+
+            def picker(idx, rows):
+                rows_iota = lax.broadcasted_iota(jnp.int32, (rows, n_edges), 0)
+                return jnp.where(rows_iota == idx, 1.0, 0.0).astype(F32)
+
+            one_hot_s = picker(send_idx, n_rcv * 8)
+            one_hot_r = picker(recv_idx, n_snd * 8)
+            take_s[...] = one_hot_s.T.astype(BF16)
+            take_r[...] = one_hot_r.T.astype(BF16)
+            put_s[...] = one_hot_s.astype(BF16)
+            put_r[...] = one_hot_r.astype(BF16)
+            loads[4].wait()
+            loads[5].wait()
+            pre[...] = dot(edges[...], w1[:d])
+
+        late = (me_r - 9) * (me_r - 10) * (me_r - 11) == 0
+        pl.when(jnp.logical_not(late))(prepare)
+
+        pl.semaphore_wait(barrier, n_snd - 1 + len(near))
+        for step in near:
+            copy_plane(node_blk, me_r, plane(step)).start()
+        send_snd(lambda o: node_blk, nodes_s, 1)
+        pl.when(late)(prepare)
+        for step in (-1, 1, -2, 2, -3, 3, -4, 4):
+            block = plane(step)
+            wait_plane(block)
+            if step < 4:
+                copy_plane(nodes_r.at[block], block, plane(4 if step < 0 else -4)).start()
+
         wait_for(recv_sem, nodes_s, n_snd, 1)
-        receiver = dot(take_r, unpack_blocks(nodes_s[...]).astype(BF16)).astype(BF16)
-        work[...] = dot(receiver, w1[2 * d :])
+        receiver = dot(take_r[...], unpack_blocks(nodes_s[...]).astype(BF16)).astype(BF16)
+        pre[...] += dot(receiver, w1[2 * d :])
+        for step in (-5, 5, -6, 6, -7, 7, -8):
+            wait_plane(plane(step))
+        sender = dot(take_s[...], unpack_blocks(nodes_r[...]).astype(BF16)).astype(BF16)
+        work[...] = dot(sender, w1[d : 2 * d])
         for start in range(0, n_edges, CHUNK):
             rows = pl.ds(start, CHUNK)
             act = pre[rows] + work[rows]
             pre[rows] = act
             hid[rows] = (act * jax.nn.sigmoid(act)).astype(BF16)
-        loads[2].wait()
+        loads[6].wait()
         work[...] = dot(hid[...], w2[...])
         for start in range(0, n_edges, CHUNK):
             rows = pl.ds(start, CHUNK)
@@ -202,13 +268,14 @@
             normed[rows] = out
             inv[rows] = scale
             hid[rows] = out.astype(BF16)
-        agg_out[...] = pack_blocks(dot(put_r, hid[...]))
-        send_all("snd", me_s, n_snd, lambda o: agg_out.at[o], agg_in, 2)
+        agg_out[...] = pack_blocks(dot(put_r[...], hid[...]))
+        send_snd(lambda o: agg_out.at[o], agg_in, 2)
         agg_in[me_s] = agg_out[me_s]
 
-        loads[3].wait()
-        loads[4].wait()
-        loads[5].wait()
+        loads[7].wait()
+        loads[8].wait()
+        loads[9].wait()
+        loads[10].wait()
         node_pre = dot(nodes_ref[...], nw1[:d])
         for start in range(0, n_edges, CHUNK):
             rows = pl.ds(start, CHUNK)
@@ -230,15 +297,15 @@
         gagg = pack_blocks(dot_t(node_gpre, nw1[d:]))
         gagg_blk[...] = gagg[0]
         gagg_in[me_s] = gagg[0]
-        send_all("snd", me_s, n_snd, lambda o: gagg_blk, gagg_in, 3)
+        send_snd(lambda o: gagg_blk, gagg_in, 3)
         direct = gno + dot_t(node_gpre, nw1[:d])
 
         wait_for(recv_sem, gagg_in, n_snd, 3)
-        work[...] = dot(take_r, unpack_blocks(gagg_in[...]).astype(BF16))
+        work[...] = dot(take_r[...], unpack_blocks(gagg_in[...]).astype(BF16))
         for start in range(0, n_edges, CHUNK):
             rows = pl.ds(start, CHUNK)
             live = (
-                lax.broadcasted_iota(jnp.int32, (CHUNK, 1), 0) + start < count_ref[0, 0]
+                lax.broadcasted_iota(jnp.int32, (CHUNK, 1), 0) + start < count_ref[...]
             )
             up = work[rows] + jnp.where(live, geo[rows].astype(F32), 0.0)
             hid[rows] = norm_backward(up, normed[rows], inv[rows]).astype(BF16)
@@ -247,13 +314,14 @@
             rows = pl.ds(start, CHUNK)
             hid[rows] = (work[rows] * slope[rows]).astype(BF16)
         send_part = dot_t(hid[...], w1[d : 2 * d]).astype(BF16)
-        rs_out[...] = pack_blocks(dot(put_s, send_part))
-        send_all("rcv", me_r, n_rcv, lambda o: rs_out.at[o], rs_in, 4)
+        rs_out[...] = pack_blocks(dot(put_s[...], send_part))
+        send_rcv(lambda o: rs_out.at[o], rs_in, 4)
         rs_in[me_r] = rs_out[me_r]
         recv_part = dot_t(hid[...], w1[2 * d :]).astype(BF16)
-        rr_out[...] = pack_blocks(dot(put_r, recv_part))
-        send_all("snd", me_s, n_snd, lambda o: rr_out.at[o], rr_in, 5)
+        rr_out[...] = pack_blocks(dot(put_r[...], recv_part))
+        send_snd(lambda o: rr_out.at[o], rr_in, 5)
         rr_in[me_s] = rr_out[me_s]
+        live_col = lax.broadcasted_iota(jnp.int32, (n_edges, 1), 0) < count_ref[...]
         gedges_ref[...] = jnp.where(live_col, geo[...].astype(F32), 0.0) + dot_t(
             hid[...], w1[:d]
         )
@@ -292,7 +360,6 @@
         n_edges, d = edges.shape[2:]
         vmem = pl.BlockSpec(memory_space=pltpu.VMEM)
         hbm = pl.BlockSpec(memory_space=pltpu.HBM)
-        smem = pl.BlockSpec(memory_space=pltpu.SMEM)
         half = d // 2
         grad_nodes, grad_edges = pl.pallas_call(
             make_kernel(n_snd, n_rcv),
@@ -300,9 +367,14 @@
                 jax.ShapeDtypeStruct(nodes.shape, F32),
                 jax.ShapeDtypeStruct((n_edges, d), F32),
             ),
-            in_specs=[smem, vmem, vmem, vmem, vmem] + [hbm] * 6,
+            in_specs=[hbm] * 11,
             out_specs=(vmem, vmem),
             scratch_shapes=[
+                pltpu.VMEM((1, 1), jnp.int32),
+                pltpu.VMEM((1, n_edges), jnp.int32),
+                pltpu.VMEM((1, n_edges), jnp.int32),
+                pltpu.VMEM(nodes.shape, BF16),
+                pltpu.VMEM(nodes.shape, BF16),
                 pltpu.VMEM((n_edges, d), BF16),
                 pltpu.VMEM((n_edges, d), BF16),
                 pltpu.VMEM(edge_w1.shape, BF16),
@@ -326,12 +398,17 @@
                 pltpu.VMEM((n_edges, d), F32),
                 pltpu.VMEM((n_edges, d), BF16),
                 pltpu.VMEM((n_edges, d), F32),
+                pltpu.VMEM((n_rcv * 8, n_edges), BF16),
+                pltpu.VMEM((n_snd * 8, n_edges), BF16),
+                pltpu.VMEM((n_edges, n_rcv * 8), BF16),
+                pltpu.VMEM((n_edges, n_snd * 8), BF16),
+                pltpu.SemaphoreType.DMA((11,)),
                 pltpu.SemaphoreType.DMA((6,)),
                 pltpu.SemaphoreType.DMA((6,)),
-                pltpu.SemaphoreType.DMA((6,)),
+                pltpu.SemaphoreType.DMA((n_rcv,)),
             ],
             compiler_params=pltpu.CompilerParams(
-                collective_id=0, has_side_effects=True, vmem_limit_bytes=48 * 1024 * 1024
+                collective_id=0, has_side_effects=True, vmem_limit_bytes=60 * 1024 * 1024
             ),
         )(
             edge_count,

time: 66.3 us -> 52.9 us (0.80)
  local copies, waits for them, and re-layouts: 10.8 us -> 3.19 us
  Pallas kernels: 53.6 us -> 48.1 us
    unnamed x22 -> x2, local copies, waits for them, and re-layouts: 10.8 us -> 3.19 us
    pallas_call x1, Pallas kernels: 53.6 us -> 48.1 us  [local(): pl.pallas_call(make_kernel(n_snd, n_rcv), out_shape=(jax.ShapeDtypeStruct...]
where the time goes in v2:
time: 52.9 us; the launch traced here: 52.6 us
  Pallas kernels  48.1 us (91%)
  local copies, waits for them, and re-layouts  3.19 us (6%)
  between operations  1.29 us (2%)
    pallas_call x1, Pallas kernels, local(): pl.pallas_call(make_kernel(n_snd, n_rcv), out_shape=(jax.ShapeDtypeStruct...  48.1 us
    unnamed x2, local copies, waits for them, and re-layouts  3.19 us

profile of v2, /device:TPU:1, one launch (start us, length us, event | category | flops | bytes accessed | tf_op | source)
XLA Modules:
  0.0 52.6 jit_solution(16548117641737700366)
XLA Ops:
  1.3 48.1 %shard_map.122 = (f32[8,512]{1,0:T(8,128)}, f32[256,512]{1,0:T(8,128)}) custom-call(s32[1,1]{1,0:T(1,128)S(6)} %copy.15.count_hbm, s32[1,256]{1,0:T(1,128)} %bitcast.8, s32[1,256]{1,0:T(1,128)} %bitcast.9, bf16[8,512]{1,0:T(8,128)(2,1)} %nodes_hbm.1, bf16[8,512]{1,0:T(8,128)(2,1)} %gno_hbm.1, bf16[256,512]{1,0:T(8,128)(2,1)} %bitcast.6, ...), custom_call_target="tpu_custom_call" | custom-call | tf_op jit(solution)/shard_map/pallas_call | solution.py:364
  49.4 1.3 %copy.16 = f32[8,512]{1,0:T(8,128)} copy(f32[8,512]{1,0:T(8,128)} %get-tuple-element.8) | data formatting | bytes 32768
  50.8 1.9 %copy.17 = f32[1,1,256,512]{3,2,1,0:T(8,128)} copy(f32[1,1,256,512]{3,2,1,0:T(8,128)} %bitcast.5) | data formatting | bytes 1048576

commit v3 on v2

--- a/solution.py
+++ b/solution.py
@@ -54,6 +54,34 @@
         upstream
         - jnp.mean(upstream, -1, keepdims=True)
         - normed * jnp.mean(upstream * normed, -1, keepdims=True)
+    )
+
+
+def hand_over(grad_nodes, grad_edges):
+    def kernel(nodes_in, edges_in, nodes_out, edges_out, sems):
+        copies = [
+            pltpu.make_async_copy(edges_in, edges_out, sems.at[0]),
+            pltpu.make_async_copy(nodes_in, nodes_out, sems.at[1]),
+        ]
+        for copy in copies:
+            copy.start()
+        for copy in copies:
+            copy.wait()
+
+    vmem = pl.BlockSpec(memory_space=pltpu.VMEM)
+    hbm = pl.BlockSpec(memory_space=pltpu.HBM)
+    return pl.pallas_call(
+        kernel,
+        out_shape=(
+            jax.ShapeDtypeStruct(grad_nodes.shape, F32),
+            jax.ShapeDtypeStruct(grad_edges.shape, F32),
+        ),
+        in_specs=[vmem, vmem],
+        out_specs=(hbm, hbm),
+        scratch_shapes=[pltpu.SemaphoreType.DMA((2,))],
+    )(
+        pltpu.with_memory_space_constraint(grad_nodes, pltpu.VMEM),
+        pltpu.with_memory_space_constraint(grad_edges, pltpu.VMEM),
     )
 
 
@@ -134,8 +162,7 @@
                 ]
             )
         ]
-        for load in loads:
-            load.start()
+        loads[0].start()
 
         barrier = pltpu.get_barrier_semaphore()
 
@@ -153,14 +180,15 @@
             )[:-1]
         ]
 
-        for other in snd_partners:
-            pl.semaphore_signal(barrier, inc=1, device_id={"snd": other}, device_id_type=MESH)
-
         near = (4, -4, 3, -3, 2, -2, 1, -1)
         for step in near:
             pl.semaphore_signal(
                 barrier, inc=1, device_id={"rcv": plane(step)}, device_id_type=MESH
             )
+        for other in snd_partners:
+            pl.semaphore_signal(barrier, inc=1, device_id={"snd": other}, device_id_type=MESH)
+        for load in loads[1:]:
+            load.start()
 
         def copy_snd(other, src, dst, k):
             return pltpu.make_async_remote_copy(
@@ -234,7 +262,7 @@
             loads[5].wait()
             pre[...] = dot(edges[...], w1[:d])
 
-        late = (me_r - 9) * (me_r - 10) * (me_r - 11) == 0
+        late = me_r >= n_rcv // 2
         pl.when(jnp.logical_not(late))(prepare)
 
         pl.semaphore_wait(barrier, n_snd - 1 + len(near))
@@ -364,8 +392,8 @@
         grad_nodes, grad_edges = pl.pallas_call(
             make_kernel(n_snd, n_rcv),
             out_shape=(
-                jax.ShapeDtypeStruct(nodes.shape, F32),
-                jax.ShapeDtypeStruct((n_edges, d), F32),
+                pltpu.VMEM(nodes.shape, F32),
+                pltpu.VMEM((n_edges, d), F32),
             ),
             in_specs=[hbm] * 11,
             out_specs=(vmem, vmem),
@@ -408,21 +436,27 @@
                 pltpu.SemaphoreType.DMA((n_rcv,)),
             ],
             compiler_params=pltpu.CompilerParams(
-                collective_id=0, has_side_effects=True, vmem_limit_bytes=60 * 1024 * 1024
+                collective_id=0, has_side_effects=True, vmem_limit_bytes=48 * 1024 * 1024
             ),
         )(
             edge_count,
-            send_local.reshape(1, n_edges),
-            recv_local.reshape(1, n_edges),
-            nodes,
-            grad_nodes_out,
-            edges.reshape(n_edges, d),
-            grad_edges_out.reshape(n_edges, d),
-            edge_w1,
-            edge_w2,
-            node_w1,
-            node_w2,
+            *(
+                pltpu.with_memory_space_constraint(operand, pltpu.HBM)
+                for operand in (
+                    send_local.reshape(1, n_edges),
+                    recv_local.reshape(1, n_edges),
+                    nodes,
+                    grad_nodes_out,
+                    edges.reshape(n_edges, d),
+                    grad_edges_out.reshape(n_edges, d),
+                    edge_w1,
+                    edge_w2,
+                    node_w1,
+                    node_w2,
+                )
+            )
         )
+        grad_nodes, grad_edges = hand_over(grad_nodes, grad_edges)
         return grad_nodes, grad_edges.reshape(1, 1, n_edges, d)
 
     in_specs = (

time: 52.9 us -> 49.6 us (0.938)
  local copies, waits for them, and re-layouts: 3.19 us -> 0 us
    unnamed x2 -> x0, local copies, waits for them, and re-layouts: 3.19 us -> none
    pallas_call x1 -> x2, Pallas kernels: 48.1 us -> 48.1 us  [the longest x1 47.3 us: local(): pl.pallas_call(make_kernel(n_snd, n_rcv), out_shape=(pltpu.VMEM(nodes.sha...]
where the time goes in v3:
time: 49.6 us; the launch traced here: 49.4 us
  Pallas kernels  48.1 us (97%)
  between operations  1.29 us (3%)
    pallas_call x1, Pallas kernels, local(): pl.pallas_call(make_kernel(n_snd, n_rcv), out_shape=(pltpu.VMEM(nodes.sha...  47.3 us

profile of v3, /device:TPU:1, one launch (start us, length us, event | category | flops | bytes accessed | tf_op | source)
XLA Modules:
  0.0 49.4 jit_solution(8476729481740780071)
XLA Ops:
  1.3 47.3 %shard_map.122 = (f32[8,512]{1,0:T(8,128)S(1)}, f32[256,512]{1,0:T(8,128)S(1)}) custom-call(s32[1,1]{1,0:T(1,128)S(6)} %copy.13.count_hbm, s32[1,256]{1,0:T(1,128)} %bitcast.7, s32[1,256]{1,0:T(1,128)} %bitcast.8, bf16[8,512]{1,0:T(8,128)(2,1)} %nodes_hbm.1, bf16[8,512]{1,0:T(8,128)(2,1)} %gno_hbm.1, bf16[256,512]{1,0:T(8,128)(2,1)} %bitcast.5, ...), custom_call_target="tpu_custom_call" | custom-call | tf_op jit(solution)/shard_map/pallas_call | solution.py:392
  48.6 0.8 %shard_map.123 = (f32[8,512]{1,0:T(8,128)}, f32[256,512]{1,0:T(8,128)}) custom-call(f32[8,512]{1,0:T(8,128)S(1)} %get-tuple-element.6.nodes_in, f32[256,512]{1,0:T(8,128)S(1)} %get-tuple-element.7.edges_in), custom_call_target="tpu_custom_call" | custom-call | tf_op jit(solution)/shard_map/pallas_call | solution.py:73

commit v4 on v3

--- a/solution.py
+++ b/solution.py
@@ -172,20 +172,22 @@
         cores = [me_s % 2, (me_s + 1) % 2]
         columns = [(me_s // 2 + dx) % 4 * 2 for dx in range(4)]
         lines = [(me_s // 8 + dy) % 4 * 8 for dy in range(4)]
-        snd_partners = [
-            lines[dy] + columns[dx] + cores[core]
-            for dy, dx, core in sorted(
-                itertools.product(range(4), range(4), range(2)),
-                key=lambda step: -min(step[0], 4 - step[0]) - min(step[1], 4 - step[1]) - step[2] / 2,
-            )[:-1]
-        ]
+        chips = sorted(
+            itertools.product(range(4), range(4)),
+            key=lambda step: -min(step[0], 4 - step[0]) - min(step[1], 4 - step[1]),
+        )
+        same_core, other_core = (
+            [lines[dy] + columns[dx] + cores[core] for dy, dx in chips] for core in range(2)
+        )
+        same_core, sibling = same_core[:-1], other_core[-1]
+        snd_partners = other_core + same_core
 
         near = (4, -4, 3, -3, 2, -2, 1, -1)
         for step in near:
             pl.semaphore_signal(
                 barrier, inc=1, device_id={"rcv": plane(step)}, device_id_type=MESH
             )
-        for other in snd_partners:
+        for other in same_core + [sibling]:
             pl.semaphore_signal(barrier, inc=1, device_id={"snd": other}, device_id_type=MESH)
         for load in loads[1:]:
             load.start()
@@ -200,13 +202,23 @@
                 device_id_type=MESH,
             )
 
+        def copy_sibling(src, block):
+            return pltpu.make_async_remote_copy(
+                src_ref=src,
+                dst_ref=nodes_s.at[block],
+                send_sem=send_sem.at[1],
+                recv_sem=recv_sem.at[0],
+                device_id={"snd": sibling},
+                device_id_type=MESH,
+            )
+
         def send_snd(src_of, dst, k):
             for other in snd_partners:
                 copy_snd(other, src_of(other), dst, k).start()
 
         def send_rcv(src_of, dst, k):
-            for step in far_first:
-                other = (me_r + step) % n_rcv
+            for rank in range(n_rcv - 1):
+                other = rank + jnp.where(rank >= me_r, 1, 0)
                 pltpu.make_async_remote_copy(
                     src_ref=src_of(other),
                     dst_ref=dst.at[me_r],
@@ -265,10 +277,12 @@
         late = me_r >= n_rcv // 2
         pl.when(jnp.logical_not(late))(prepare)
 
-        pl.semaphore_wait(barrier, n_snd - 1 + len(near))
+        pl.semaphore_wait(barrier, len(near) + len(same_core) + 1)
         for step in near:
             copy_plane(node_blk, me_r, plane(step)).start()
-        send_snd(lambda o: node_blk, nodes_s, 1)
+        for other in same_core:
+            copy_snd(other, node_blk, nodes_s, 1).start()
+        copy_sibling(node_blk, me_s).start()
         pl.when(late)(prepare)
         for step in (-1, 1, -2, 2, -3, 3, -4, 4):
             block = plane(step)
@@ -276,7 +290,10 @@
             if step < 4:
                 copy_plane(nodes_r.at[block], block, plane(4 if step < 0 else -4)).start()
 
-        wait_for(recv_sem, nodes_s, n_snd, 1)
+        wait_for(recv_sem, nodes_s, n_snd // 2, 1)
+        for block in same_core:
+            copy_sibling(nodes_s.at[block], block).start()
+        wait_for(recv_sem, nodes_s, n_snd // 2 + 1, 0)
         receiver = dot(take_r[...], unpack_blocks(nodes_s[...]).astype(BF16)).astype(BF16)
         pre[...] += dot(receiver, w1[2 * d :])
         for step in (-5, 5, -6, 6, -7, 7, -8):
@@ -341,8 +358,8 @@
         for start in range(0, n_edges, CHUNK):
             rows = pl.ds(start, CHUNK)
             hid[rows] = (work[rows] * slope[rows]).astype(BF16)
-        send_part = dot_t(hid[...], w1[d : 2 * d]).astype(BF16)
-        rs_out[...] = pack_blocks(dot(put_s[...], send_part))
+        send_part = dot(put_s[...], hid[...]).astype(BF16)
+        rs_out[...] = pack_blocks(dot_t(send_part, w1[d : 2 * d]))
         send_rcv(lambda o: rs_out.at[o], rs_in, 4)
         rs_in[me_r] = rs_out[me_r]
         recv_part = dot_t(hid[...], w1[2 * d :]).astype(BF16)

time: 49.6 us -> 48 us (0.968); the launches traced: 49.4 us -> 47.3 us
  Pallas kernels: 48.1 us -> 46 us
    pallas_call x1, Pallas kernels: 47.3 us -> 45.2 us  [local(): pl.pallas_call(make_kernel(n_snd, n_rcv), out_shape=(pltpu.VMEM(nodes.sha...]
where the time goes in v4:
time: 48 us; the launch traced here: 47.3 us
  Pallas kernels  46 us (96%)
  between operations  1.29 us (3%)
    pallas_call x1, Pallas kernels, local(): pl.pallas_call(make_kernel(n_snd, n_rcv), out_shape=(pltpu.VMEM(nodes.sha...  45.2 us

profile of v4, /device:TPU:1, one launch (start us, length us, event | category | flops | bytes accessed | tf_op | source)
XLA Modules:
  0.0 47.3 jit_solution(16465977505843843252)
XLA Ops:
  1.3 45.2 %shard_map.122 = (f32[8,512]{1,0:T(8,128)S(1)}, f32[256,512]{1,0:T(8,128)S(1)}) custom-call(s32[1,1]{1,0:T(1,128)S(6)} %copy.13.count_hbm, s32[1,256]{1,0:T(1,128)} %bitcast.7, s32[1,256]{1,0:T(1,128)} %bitcast.8, bf16[8,512]{1,0:T(8,128)(2,1)} %nodes_hbm.1, bf16[8,512]{1,0:T(8,128)(2,1)} %gno_hbm.1, bf16[256,512]{1,0:T(8,128)(2,1)} %bitcast.5, ...), custom_call_target="tpu_custom_call" | custom-call | tf_op jit(solution)/shard_map/pallas_call | solution.py:409
  46.5 0.8 %shard_map.123 = (f32[8,512]{1,0:T(8,128)}, f32[256,512]{1,0:T(8,128)}) custom-call(f32[8,512]{1,0:T(8,128)S(1)} %get-tuple-element.6.nodes_in, f32[256,512]{1,0:T(8,128)S(1)} %get-tuple-element.7.edges_in), custom_call_target="tpu_custom_call" | custom-call | tf_op jit(solution)/shard_map/pallas_call | solution.py:73

commit v5 on v4

--- a/solution.py
+++ b/solution.py
@@ -138,6 +138,7 @@
         send_sem,
         recv_sem,
         plane_sem,
+        turn_sem,
     ):
         me_s = lax.axis_index("snd")
         me_r = lax.axis_index("rcv")
@@ -180,14 +181,17 @@
             [lines[dy] + columns[dx] + cores[core] for dy, dx in chips] for core in range(2)
         )
         same_core, sibling = same_core[:-1], other_core[-1]
+        greeted = same_core[1:]
+        two_lines, two_columns = (same_core[chips.index(chip)] for chip in ((2, 0), (0, 2)))
         snd_partners = other_core + same_core
 
-        near = (4, -4, 3, -3, 2, -2, 1, -1)
+        near = (3, -3, 2, -2, 1, -1)
+        passed = ((-2, (2,)), (2, (-2,)), (-3, (5, 4, 3, 2)), (3, (-4, -3, -2)))
         for step in near:
             pl.semaphore_signal(
                 barrier, inc=1, device_id={"rcv": plane(step)}, device_id_type=MESH
             )
-        for other in same_core + [sibling]:
+        for other in greeted + [sibling]:
             pl.semaphore_signal(barrier, inc=1, device_id={"snd": other}, device_id_type=MESH)
         for load in loads[1:]:
             load.start()
@@ -198,6 +202,16 @@
                 dst_ref=dst.at[me_s],
                 send_sem=send_sem.at[k],
                 recv_sem=recv_sem.at[k],
+                device_id={"snd": other},
+                device_id_type=MESH,
+            )
+
+        def copy_turn(other, src, block, turn):
+            return pltpu.make_async_remote_copy(
+                src_ref=src,
+                dst_ref=nodes_s.at[block],
+                send_sem=send_sem.at[1],
+                recv_sem=turn_sem if turn else recv_sem.at[1],
                 device_id={"snd": other},
                 device_id_type=MESH,
             )
@@ -277,26 +291,32 @@
         late = me_r >= n_rcv // 2
         pl.when(jnp.logical_not(late))(prepare)
 
-        pl.semaphore_wait(barrier, len(near) + len(same_core) + 1)
+        pl.semaphore_wait(barrier, len(near) + len(greeted) + 1)
         for step in near:
             copy_plane(node_blk, me_r, plane(step)).start()
-        for other in same_core:
-            copy_snd(other, node_blk, nodes_s, 1).start()
+        for other in greeted:
+            if other is two_columns:
+                copy_turn(other, node_blk, me_s, 1).start()
+            else:
+                copy_snd(other, node_blk, nodes_s, 1).start()
         copy_sibling(node_blk, me_s).start()
         pl.when(late)(prepare)
-        for step in (-1, 1, -2, 2, -3, 3, -4, 4):
+        for step, passes in passed:
             block = plane(step)
             wait_plane(block)
-            if step < 4:
-                copy_plane(nodes_r.at[block], block, plane(4 if step < 0 else -4)).start()
-
-        wait_for(recv_sem, nodes_s, n_snd // 2, 1)
+            for to in passes:
+                copy_plane(nodes_r.at[block], block, plane(to)).start()
+            if step == 2:
+                pltpu.make_async_copy(node_blk, nodes_s.at[two_columns], turn_sem).wait()
+                copy_turn(two_lines, nodes_s.at[two_columns], two_columns, 0).start()
+
+        wait_for(recv_sem, nodes_s, n_snd // 2 - 1, 1)
         for block in same_core:
             copy_sibling(nodes_s.at[block], block).start()
         wait_for(recv_sem, nodes_s, n_snd // 2 + 1, 0)
         receiver = dot(take_r[...], unpack_blocks(nodes_s[...]).astype(BF16)).astype(BF16)
         pre[...] += dot(receiver, w1[2 * d :])
-        for step in (-5, 5, -6, 6, -7, 7, -8):
+        for step in (-1, 1, -4, 4, -5, 5, -6, 6, -7, 7, -8):
             wait_plane(plane(step))
         sender = dot(take_s[...], unpack_blocks(nodes_r[...]).astype(BF16)).astype(BF16)
         work[...] = dot(sender, w1[d : 2 * d])
@@ -451,6 +471,7 @@
                 pltpu.SemaphoreType.DMA((6,)),
                 pltpu.SemaphoreType.DMA((6,)),
                 pltpu.SemaphoreType.DMA((n_rcv,)),
+                pltpu.SemaphoreType.DMA,
             ],
             compiler_params=pltpu.CompilerParams(
                 collective_id=0, has_side_effects=True, vmem_limit_bytes=48 * 1024 * 1024

time: 48 us -> 47.4 us (0.987)
  no operation moved by 1% of the time
where the time goes in v5:
time: 47.4 us; the launch traced here: 47 us
  Pallas kernels  45.8 us (97%)
  between operations  1.29 us (3%)
    pallas_call x1, Pallas kernels, local(): pl.pallas_call(make_kernel(n_snd, n_rcv), out_shape=(pltpu.VMEM(nodes.sha...  44.9 us

profile of v5, /device:TPU:1, one launch (start us, length us, event | category | flops | bytes accessed | tf_op | source)
XLA Modules:
  0.0 47.0 jit_solution(1978252524127647816)
XLA Ops:
  1.3 44.9 %shard_map.122 = (f32[8,512]{1,0:T(8,128)S(1)}, f32[256,512]{1,0:T(8,128)S(1)}) custom-call(s32[1,1]{1,0:T(1,128)S(6)} %copy.13.count_hbm, s32[1,256]{1,0:T(1,128)} %bitcast.7, s32[1,256]{1,0:T(1,128)} %bitcast.8, bf16[8,512]{1,0:T(8,128)(2,1)} %nodes_hbm.1, bf16[8,512]{1,0:T(8,128)(2,1)} %gno_hbm.1, bf16[256,512]{1,0:T(8,128)(2,1)} %bitcast.5, ...), custom_call_target="tpu_custom_call" | custom-call | tf_op jit(solution)/shard_map/pallas_call | solution.py:429
  46.2 0.8 %shard_map.123 = (f32[8,512]{1,0:T(8,128)}, f32[256,512]{1,0:T(8,128)}) custom-call(f32[8,512]{1,0:T(8,128)S(1)} %get-tuple-element.6.nodes_in, f32[256,512]{1,0:T(8,128)S(1)} %get-tuple-element.7.edges_in), custom_call_target="tpu_custom_call" | custom-call | tf_op jit(solution)/shard_map/pallas_call | solution.py:73

commit v6 on v5

--- a/solution.py
+++ b/solution.py
@@ -347,6 +347,8 @@
             act = pre[rows]
             sigma = jax.nn.sigmoid(act)
             slope[rows] = sigma * (1.0 + act * (1.0 - sigma))
+        live_col = lax.broadcasted_iota(jnp.int32, (n_edges, 1), 0) < count_ref[...]
+        gedges_ref[...] = jnp.where(live_col, geo[...].astype(F32), 0.0)
 
         wait_for(recv_sem, agg_in, n_snd, 2)
         aggregate = unpack_sum(agg_in[...]).astype(BF16)
@@ -369,10 +371,7 @@
         work[...] = dot(take_r[...], unpack_blocks(gagg_in[...]).astype(BF16))
         for start in range(0, n_edges, CHUNK):
             rows = pl.ds(start, CHUNK)
-            live = (
-                lax.broadcasted_iota(jnp.int32, (CHUNK, 1), 0) + start < count_ref[...]
-            )
-            up = work[rows] + jnp.where(live, geo[rows].astype(F32), 0.0)
+            up = work[rows] + gedges_ref[rows]
             hid[rows] = norm_backward(up, normed[rows], inv[rows]).astype(BF16)
         work[...] = dot_t(hid[...], w2[...])
         for start in range(0, n_edges, CHUNK):
@@ -386,10 +385,7 @@
         rr_out[...] = pack_blocks(dot(put_r[...], recv_part))
         send_snd(lambda o: rr_out.at[o], rr_in, 5)
         rr_in[me_s] = rr_out[me_s]
-        live_col = lax.broadcasted_iota(jnp.int32, (n_edges, 1), 0) < count_ref[...]
-        gedges_ref[...] = jnp.where(live_col, geo[...].astype(F32), 0.0) + dot_t(
-            hid[...], w1[:d]
-        )
+        gedges_ref[...] += dot_t(hid[...], w1[:d])
 
         wait_for(recv_sem, rr_in, n_snd, 5)
         direct = direct + unpack_sum(rr_in[...])

time: 47.4 us -> 47.3 us (level)
  no operation moved by 1% of the time
where the time goes in v6:
time: 47.3 us; the launch traced here: 46.9 us
  Pallas kernels  45.6 us (96%)
  between operations  1.29 us (3%)
    pallas_call x1, Pallas kernels, local(): pl.pallas_call(make_kernel(n_snd, n_rcv), out_shape=(pltpu.VMEM(nodes.sha...  44.8 us

profile of v6, /device:TPU:1, one launch (start us, length us, event | category | flops | bytes accessed | tf_op | source)
XLA Modules:
  0.0 46.9 jit_solution(16079365302042803351)
XLA Ops:
  1.3 44.8 %shard_map.122 = (f32[8,512]{1,0:T(8,128)S(1)}, f32[256,512]{1,0:T(8,128)S(1)}) custom-call(s32[1,1]{1,0:T(1,128)S(6)} %copy.13.count_hbm, s32[1,256]{1,0:T(1,128)} %bitcast.7, s32[1,256]{1,0:T(1,128)} %bitcast.8, bf16[8,512]{1,0:T(8,128)(2,1)} %nodes_hbm.1, bf16[8,512]{1,0:T(8,128)(2,1)} %gno_hbm.1, bf16[256,512]{1,0:T(8,128)(2,1)} %bitcast.5, ...), custom_call_target="tpu_custom_call" | custom-call | tf_op jit(solution)/shard_map/pallas_call | solution.py:425
  46.1 0.8 %shard_map.123 = (f32[8,512]{1,0:T(8,128)}, f32[256,512]{1,0:T(8,128)}) custom-call(f32[8,512]{1,0:T(8,128)S(1)} %get-tuple-element.6.nodes_in, f32[256,512]{1,0:T(8,128)S(1)} %get-tuple-element.7.edges_in), custom_call_target="tpu_custom_call" | custom-call | tf_op jit(solution)/shard_map/pallas_call | solution.py:73

commit v7 on v6

--- a/solution.py
+++ b/solution.py
@@ -186,7 +186,7 @@
         snd_partners = other_core + same_core
 
         near = (3, -3, 2, -2, 1, -1)
-        passed = ((-2, (2,)), (2, (-2,)), (-3, (5, 4, 3, 2)), (3, (-4, -3, -2)))
+        passed = ((-2, (2,)), (2, (-2,)), (-3, (4, 3, 2)), (3, (-4, -3, -2)))
         for step in near:
             pl.semaphore_signal(
                 barrier, inc=1, device_id={"rcv": plane(step)}, device_id_type=MESH
@@ -304,6 +304,10 @@
         for step, passes in passed:
             block = plane(step)
             wait_plane(block)
+            if step == 3:
+                sign = 1 - 2 * (me_r % 2)
+                far = plane(-3 * sign)
+                copy_plane(nodes_r.at[far], far, plane(5 * sign)).start()
             for to in passes:
                 copy_plane(nodes_r.at[block], block, plane(to)).start()
             if step == 2:

time: 47.3 us -> 47.9 us (1.013)
  no operation moved by 1% of the time
where the time goes in v7:
time: 47.9 us; the launch traced here: 47.1 us
  Pallas kernels  45.8 us (96%)
  between operations  1.29 us (3%)
    pallas_call x1, Pallas kernels, local(): pl.pallas_call(make_kernel(n_snd, n_rcv), out_shape=(pltpu.VMEM(nodes.sha...  45 us

profile of v7, /device:TPU:1, one launch (start us, length us, event | category | flops | bytes accessed | tf_op | source)
XLA Modules:
  0.0 47.1 jit_solution(4090551954711175306)
XLA Ops:
  1.3 45.0 %shard_map.122 = (f32[8,512]{1,0:T(8,128)S(1)}, f32[256,512]{1,0:T(8,128)S(1)}) custom-call(s32[1,1]{1,0:T(1,128)S(6)} %copy.13.count_hbm, s32[1,256]{1,0:T(1,128)} %bitcast.7, s32[1,256]{1,0:T(1,128)} %bitcast.8, bf16[8,512]{1,0:T(8,128)(2,1)} %nodes_hbm.1, bf16[8,512]{1,0:T(8,128)(2,1)} %gno_hbm.1, bf16[256,512]{1,0:T(8,128)(2,1)} %bitcast.5, ...), custom_call_target="tpu_custom_call" | custom-call | tf_op jit(solution)/shard_map/pallas_call | solution.py:429
  46.2 0.8 %shard_map.123 = (f32[8,512]{1,0:T(8,128)}, f32[256,512]{1,0:T(8,128)}) custom-call(f32[8,512]{1,0:T(8,128)S(1)} %get-tuple-element.6.nodes_in, f32[256,512]{1,0:T(8,128)S(1)} %get-tuple-element.7.edges_in), custom_call_target="tpu_custom_call" | custom-call | tf_op jit(solution)/shard_map/pallas_call | solution.py:73
